TPU v7x, 512 devices: a whole 4x4x16 slice. The times are simulated.
512 devices in a mesh: gx: 4 (over y), gy: 8 (over x, core), gz: 16 (over z).
Axes of the slice: x: 4, y: 4, z: 16, core: 2. Of those that a mesh axis runs over, the one named last changes fastest.
Arguments:
- right_side: float32 [64, 256, 2048], P('gx', 'gy', 'gz'), may hold values from -24 to 24
- face_x: float32 [64, 256, 2048], P('gx', 'gy', 'gz'), may hold values from 0.2 to 5
- face_y: float32 [64, 256, 2048], P('gx', 'gy', 'gz'), may hold values from 0.2 to 5
- face_z: float32 [64, 256, 2048], P('gx', 'gy', 'gz'), may hold values from 0.2 to 5
- absorb: float32 [64, 256, 2048], P('gx', 'gy', 'gz'), may hold values from 0.02 to 0.2
Outputs:
- solution: float32 [64, 256, 2048], P('gx', 'gy', 'gz')
All inputs are finite; a program needn't handle non-finite values.
Results may differ from a plain program's by a relative error of at most 0.00002.
Values sent between devices are 32-bit elements; how exact they have to be, the bound alone decides.
A program may use at most 64 MiB of HBM per device.

v0:
```python
import functools

import jax
import jax.numpy as jnp
from jax import lax
from jax.experimental import pallas as pl
from jax.experimental.pallas import tpu as pltpu
from jax.sharding import PartitionSpec as P

MESH = pl.DeviceIdType.MESH
F32 = jnp.float32
HI = lax.Precision.HIGHEST

B, S, FY, FZ, FX = range(5)

ALL26 = sorted(
    [(a, b, c) for a in (-1, 0, 1) for b in (-1, 0, 1) for c in (-1, 0, 1) if (a, b, c) != (0, 0, 0)],
    key=lambda d: -sum(map(abs, d)),
)


def cheb_factors(steps, lowest, highest):
    centre = 0.5 * (lowest + highest)
    half = 0.5 * (highest - lowest)
    q = centre / half
    rho = 1.0 / q
    out = []
    for _ in range(steps - 1):
        nxt = 1.0 / (2.0 * q - rho)
        out.append((nxt * rho, 2.0 * nxt / half))
        rho = nxt
    return 1.0 / centre, out


def iota(shape, dim):
    return lax.broadcasted_iota(jnp.int32, shape, dim)


def dot(a, b):
    return jnp.dot(a, b, precision=HI, preferred_element_type=F32)


def shift(v, amount, axis):
    return pltpu.roll(v, amount % v.shape[axis], axis)


def restrict_weights(z, k, ok):
    t = z - 2 * k
    w = jnp.where((t == 0) | (t == 1), 0.375, jnp.where((t == -1) | (t == 2), 0.125, 0.0))
    return jnp.where(ok, w, 0.0)


def prolong_weights(coarse, fine):
    k = fine >> 1
    side = jnp.where((fine & 1) == 0, k - 1, k + 1)
    return jnp.where(coarse == k, 0.75, jnp.where(coarse == side, 0.25, 0.0))


def kernel(sizes, b_in, fx_in, fy_in, fz_in, s_in, out,
           C, ID, V, D, W, RX, ZC, LC, ZV, LV,
           KP, K1, ZK, LK, B1, I1, X1, D1, T1, ZB, LB, RX1,
           K2P, LK2, B2P, LB2, K2, I2, X2, D2, Y2, PY1, PY0,
           in_sem, c_s, c_r, v_s, v_r, k_s, k_r, b_s, b_r, k2_s, k2_r, b2_s, b2_r):
    GX, GY, GZ = sizes
    gx, gy, gz = (lax.axis_index(a) for a in ("gx", "gy", "gz"))
    me = (gx, gy, gz)

    def dev(d):
        return tuple(lax.rem(m + (q + s), s) for m, q, s in zip(me, d, sizes))

    loads = []
    for f, ref in ((B, b_in), (S, s_in), (FX, fx_in), (FY, fy_in), (FZ, fz_in)):
        c = pltpu.make_async_copy(ref, C.at[f, 0, pl.ds(2, 16), pl.ds(8, 32)], in_sem.at[f])
        c.start()
        loads.append(c)

    far = [(a, b, c) for a in range(GX) for b in (-1, 0, 1) for c in (-1, 0, 1) if (a, b, c) != (0, 0, 0)]
    far = sorted(far, key=lambda d: -(min(d[0], GX - d[0]) + abs(d[1]) + abs(d[2])))
    bar = pltpu.get_barrier_semaphore()
    for d in far:
        pl.semaphore_signal(bar, inc=1, device_id=dev(d), device_id_type=MESH)

    def start(msgs, ss, rs):
        copies = []
        for k, (d, src, dst) in enumerate(msgs):
            c = pltpu.make_async_remote_copy(
                src_ref=src, dst_ref=dst, send_sem=ss.at[k], recv_sem=rs.at[k],
                device_id=dev(d), device_id_type=MESH)
            c.start()
            copies.append(c)
        return copies

    def finish(copies):
        for c in copies:
            c.wait_recv()
        for c in copies:
            c.wait_send()

    lane128 = iota((1, 128), 1)
    first = [m == 0 for m in me]
    last = [m == s - 1 for m, s in zip(me, sizes)]

    for c in loads:
        c.wait()

    C[FX, 0, 17, 8:40, :] = jnp.where(last[0], 0.0, C[FX, 0, 17, 8:40, :])
    row8 = iota((8, 128), 0)
    lane32 = iota((32, 128), 1)

    def close(x, _):
        C[FY, 0, x, 32:40, :] = jnp.where(last[1] & (row8 == 7), 0.0, C[FY, 0, x, 32:40, :])
        C[FZ, 0, x, 8:40, :] = jnp.where(last[2] & (lane32 == 127), 0.0, C[FZ, 0, x, 8:40, :])
        return 0

    lax.fori_loop(2, 18, close, 0)

    TILES = ((0, 6), (6, 5), (11, 5))

    for t, (x0, n) in enumerate(TILES):
        def pack(i, acc, x0=x0):
            for f in range(5):
                g = i * 5 + f
                v = pltpu.roll(C[f, 0, 2 + x0 + i, 8:40, :], 4 * g + 2, 1)
                acc = jnp.where((lane32 >> 2) == g, v, acc)
            return acc
        ZC[t] = lax.fori_loop(0, n, pack, jnp.zeros((32, 128), F32))

    pl.semaphore_wait(bar, len(far))

    ROWS = {1: (32, 0, 8), -1: (8, 40, 8), 0: (8, 8, 32)}

    def fine_msgs(dirs, xs, field, zsrc, zland, ztiles):
        msgs = []
        for d in dirs:
            dx, dy, dz = d
            sy, ty, ny = ROWS[dy]
            if dz == 0:
                sx, tx, nx = xs[dx]
                msgs.append((d, field(pl.ds(sx, nx), pl.ds(sy, ny)), field(pl.ds(tx, nx), pl.ds(ty, ny))))
            else:
                side = 0 if dz == 1 else 1
                s0, t0, nt = ztiles[dx]
                msgs.append((d, zsrc.at[pl.ds(s0, nt), pl.ds(sy - 8, ny)], zland.at[side, pl.ds(t0, nt), pl.ds(ty, ny)]))
        return msgs

    cfield = lambda xs, ys: C.at[:, 0, xs, ys]
    c_msgs = fine_msgs(ALL26, {1: (17, 1, 1), -1: (2, 18, 1), 0: (2, 2, 16)}, cfield, ZC, LC,
                       {1: (2, 0, 1), 0: (0, 1, 3), -1: (0, 4, 1)})
    for dy in (-1, 0, 1):
        sy, ty, ny = ROWS[dy]
        c_msgs.append(((1, dy, 0), C.at[FX, 0, pl.ds(16, 1), pl.ds(sy, ny)], C.at[FX, 0, pl.ds(0, 1), pl.ds(ty, ny)]))
    c_copies = start(c_msgs, c_s, c_r)

    li, lo = iota((256, 128), 0), iota((256, 128), 1)
    hit = ((li & 127) >> 1) == (lo & 63)
    hit = hit & ((li >> 7) == (lo >> 6))
    odd = (li & 1) == 1
    wa = jnp.where(hit, 1.0 / 16, 0.0)
    wb = jnp.where(li < 128, jnp.where(hit & odd, 1.0 / 16, 0.0), jnp.where(hit, 1.0 / 8, 0.0))

    def mid(i, _):
        x = 2 + 2 * i
        ev, od = pl.ds(8, 16, stride=2), pl.ds(9, 16, stride=2)
        mx = C[FX, 0, x + 1, ev, :] + C[FX, 0, x + 1, od, :]
        my = C[FY, 0, x, od, :] + C[FY, 0, x + 1, od, :]
        mz = (C[FZ, 0, x, ev, :] + C[FZ, 0, x, od, :]) + (C[FZ, 0, x + 1, ev, :] + C[FZ, 0, x + 1, od, :])
        ms = (C[S, 0, x, ev, :] + C[S, 0, x, od, :]) + (C[S, 0, x + 1, ev, :] + C[S, 0, x + 1, od, :])
        RX[0, i, 0:16, :] = mx
        RX[1, i, 0:16, :] = my
        RX[0, i, 16:32, :] = mz
        RX[1, i, 16:32, :] = ms
        return 0

    lax.fori_loop(0, 8, mid, 0)
    for p, w in ((0, wa), (1, wb)):
        lhs = jnp.concatenate(
            [RX[q, :, 16 * p:16 * p + 16, :].reshape(128, 128) for q in (0, 1)], axis=1)
        KP[p, 6:14, 8:24, :] = dot(lhs, w).reshape(8, 16, 128)

    lane16 = iota((16, 128), 1)

    def pack_mid(load, base):
        acc = jnp.zeros((16, 128), F32)
        for x in range(8):
            v = load(x)
            acc = jnp.where((lane16 >> 3) == 2 * x, shift(v, 16 * x - (base + 56), 1), acc)
            acc = jnp.where((lane16 >> 3) == 2 * x + 1, shift(v, 16 * x + 8 - base, 1), acc)
        return acc

    for f in range(4):
        ZK[f] = pack_mid(lambda x: KP[f // 2, 6 + x, 8:24, :], 64 * (f % 2))

    MROWS = {1: (16, 0, 8), -1: (8, 24, 8), 0: (8, 8, 16)}

    def mid_msgs(xs, field, zsrc, zland):
        msgs = []
        for d in ALL26:
            dx, dy, dz = d
            sy, ty, ny = MROWS[dy]
            if dz == 0:
                sx, tx, nx = xs[dx]
                msgs.append((d, field(pl.ds(sx, nx), pl.ds(sy, ny)), field(pl.ds(tx, nx), pl.ds(ty, ny))))
            else:
                side = 0 if dz == 1 else 1
                msgs.append((d, zsrc(pl.ds(sy - 8, ny)), zland(side, 1 - dx, pl.ds(ty, ny))))
        return msgs

    finish(c_copies)

    k_copies = start(
        mid_msgs({1: (8, 0, 6), -1: (6, 14, 5), 0: (6, 6, 8)},
                 lambda xs, ys: KP.at[:, xs, ys],
                 lambda ys: ZK.at[:, ys], lambda side, j, ys: LK.at[side, j, :, ys]), k_s, k_r)

    lane48 = iota((48, 128), 1)
    for j, (x0, n, i0) in enumerate(((0, 2, 3), (2, 6, 0), (8, 5, 0), (13, 5, 0), (18, 2, 0))):
        both = jnp.where((lane48 & 3) >= 2, LC[1, j], LC[0, j])
        LC[0, j] = both

        def spread(i, _, j=j, x0=x0, i0=i0):
            both = LC[0, j]
            for f in range(5):
                C[f, 1, x0 + i, :, :] = pltpu.roll(both, 126 + 128 - 4 * ((i + i0) * 5 + f), 1)
            return 0

        lax.fori_loop(0, n, spread, 0)

    def ld(ref, x):
        return jnp.concatenate([ref[0, x], ref[1, x]], axis=1)

    def ldc(f, x):
        return jnp.concatenate([C[f, 0, x], C[f, 1, x]], axis=1)

    def st(ref, x, v):
        ref[0, x] = v[:, :128]
        ref[1, x] = v[:, 128:]

    t_inv, ((ca, cb),) = cheb_factors(2, 0.5, 2.0)

    def diag0(x, _):
        fy, fz = ldc(FY, x), ldc(FZ, x)
        diag = (ldc(S, x) + ldc(FX, x) + ldc(FX, x - 1)) + (fy + shift(fy, 1, 0)) + (fz + shift(fz, 1, 1))
        inv = 1.0 / diag
        st(ID, x, inv)
        st(D, x, t_inv * inv * ldc(B, x))
        return 0

    lax.fori_loop(1, 19, diag0, 0)

    def residual0(ref, x):
        v = ld(ref, x)
        gy_ = ldc(FY, x) * (v - shift(v, -1, 0))
        gz_ = ldc(FZ, x) * (v - shift(v, -1, 1))
        av = ldc(S, x) * v + ldc(FX, x) * (v - ld(ref, x + 1)) + ldc(FX, x - 1) * (v - ld(ref, x - 1))
        av = av + (gy_ - shift(gy_, 1, 0)) + (gz_ - shift(gz_, 1, 1))
        return v, ldc(B, x) - av

    def pre0(x, _):
        d, r = residual0(D, x)
        v = d + (ca * d + cb * ld(ID, x) * r)
        V[0, x, 8:40, :] = v[8:40, :128]
        return 0

    lax.fori_loop(2, 18, pre0, 0)

    def pack_v(i, acc):
        v = pltpu.roll(V[0, 2 + i, 8:40, :], 4 * i + 2, 1)
        return jnp.where((lane32 >> 2) == i, v, acc)

    ZV[0] = lax.fori_loop(0, 16, pack_v, jnp.zeros((32, 128), F32))
    v_copies = start(
        fine_msgs(ALL26, {1: (16, 0, 2), -1: (2, 18, 2), 0: (2, 2, 16)},
                  lambda xs, ys: V.at[0, xs, ys], ZV, LV, {1: (0, 0, 1), 0: (0, 1, 1), -1: (0, 2, 1)}), v_s, v_r)

    wi, wo = iota((128, 128), 0), iota((128, 128), 1)
    in32 = wo < 32

    def packed(rows, w):
        r = dot(rows, w)
        acc = r[0:8]
        for i in range(1, 4):
            acc = acc + shift(r[8 * i:8 * i + 8], 32 * i, 1)
        return acc

    for f, half in ((0, 0), (1, 64), (2, 0), (3, 64)):
        p = f // 2
        rows = []
        for i in range(4):
            x = 6 + 2 * i
            e0, o0 = KP[p, x, pl.ds(8, 8, stride=2), :], KP[p, x, pl.ds(9, 8, stride=2), :]
            e1, o1 = KP[p, x + 1, pl.ds(8, 8, stride=2), :], KP[p, x + 1, pl.ds(9, 8, stride=2), :]
            rows.append((e1 + o1) if f == 0 else (o0 + o1) if f == 1 else (e0 + o0) + (e1 + o1))
        z = wi - half
        sel = (z >= 0) & (z < 64) & ((z >> 1) == wo) & in32
        if f == 2:
            sel = sel & ((z & 1) == 1)
        K2P[f] = packed(jnp.concatenate(rows, 0), jnp.where(sel, 1.0 / (8 if f == 3 else 16), 0.0))
    rim = [C[FY, 0, 2 + x, 7:8, :] for x in range(16)]
    rim = jnp.concatenate(
        [jnp.broadcast_to((rim[4 * i] + rim[4 * i + 1]) + (rim[4 * i + 2] + rim[4 * i + 3]), (8, 128)) for i in range(4)], 0)
    below = packed(rim, jnp.where(((wi >> 2) == wo) & in32, 1.0 / 256, 0.0))
    K2P[4] = jnp.where(row8 == 0, below, shift(K2P[1], 1, 0))

    def far_msgs(src, land):
        return [(d, src, land(gx, 1 - d[2], pl.ds(8 - 8 * d[1], 8))) for d in far]

    k2_copies = start(far_msgs(K2P, lambda g, j, ys: LK2.at[g, j, :, ys]), k2_s, k2_r)
    LK2[gx, 1, :, 8:16, :] = K2P[...]

    finish(v_copies)
    for j, (x0, n, i0) in enumerate(((0, 2, 14), (2, 16, 0), (18, 2, 0))):
        LV[0, j] = jnp.where((lane48 & 3) >= 2, LV[1, j], LV[0, j])

        def spread_v(i, _, j=j, x0=x0, i0=i0):
            V[1, x0 + i, :, :] = pltpu.roll(LV[0, j], 126 + 128 - 4 * (i + i0), 1)
            return 0

        lax.fori_loop(0, n, spread_v, 0)

    r48, l256 = iota((48, 256), 0), iota((48, 256), 1)
    keep0 = ((r48 >= jnp.where(first[1], 8, 7)) & (r48 < jnp.where(last[1], 40, 41))
             & ((l256 < jnp.where(last[2], 128, 129)) | (l256 > jnp.where(first[2], 255, 254))))

    def res0(x, _):
        _, r = residual0(V, x)
        inside = ((x > 1) | jnp.logical_not(first[0])) & ((x < 18) | jnp.logical_not(last[0]))
        st(D, x, jnp.where(keep0 & inside, r, 0.0))
        return 0

    lax.fori_loop(1, 19, res0, 0)

    def rest0(i, _):
        x = 2 + 2 * i
        v = 0.125 * (ld(D, x - 1) + ld(D, x + 2)) + 0.375 * (ld(D, x) + ld(D, x + 1))
        st(RX, i, v)
        for h in (0, 1):
            rows = [RX[h, i, pl.ds(7 + k, 16, stride=2), :] for k in range(4)]
            RX[h, i, 0:16, :] = 0.125 * (rows[0] + rows[3]) + 0.375 * (rows[1] + rows[2])
        return 0

    lax.fori_loop(0, 8, rest0, 0)
    zin = jnp.where(li < 192, li, li - 256)
    wr = restrict_weights(zin, lo - 32, (lo >= 32) & (lo < 96))
    lhs = jnp.concatenate([RX[h, :, 0:16, :].reshape(128, 128) for h in (0, 1)], axis=1)
    B1[6:14, 8:24, :] = dot(lhs, wr).reshape(8, 16, 128)
    ZB[...] = pack_mid(lambda x: B1[6 + x, 8:24, :], 32)
    b_copies = start(
        mid_msgs({1: (9, 1, 5), -1: (6, 14, 5), 0: (6, 6, 8)},
                 lambda xs, ys: B1.at[xs, ys],
                 lambda ys: ZB.at[ys], lambda side, j, ys: LB.at[side, j, ys]), b_s, b_r)

    finish(k_copies)
    lane32r = iota((32, 128), 1)

    def z_halo(lm, lp, own, q):
        low = pltpu.roll(lm, 24 + 128 - 16 * q, 1)
        high = pltpu.roll(lp, 88 + 128 - 16 * q, 1)
        return jnp.where(lane32r < 32, low, jnp.where(lane32r < 96, own, high))

    MID = ((0, 0, 6, 2), (1, 6, 8, 0), (2, 14, 5, 0))
    for j, x0, n, i0 in MID:
        def spread_k(i, _, j=j, x0=x0, i0=i0):
            for f in range(4):
                own = pltpu.roll(KP[f // 2, x0 + i], 32 if f % 2 == 0 else 96, 1)
                K1[f, x0 + i] = z_halo(LK[0, j, f], LK[1, j, f], own, i + i0)
            return 0

        lax.fori_loop(0, n, spread_k, 0)

    def diag1(x, _):
        fy, fz = K1[1, x], K1[2, x]
        diag = (K1[3, x] + K1[0, x] + K1[0, x - 1]) + (fy + shift(fy, 1, 0)) + (fz + shift(fz, 1, 1))
        I1[x] = 1.0 / diag
        return 0

    lax.fori_loop(1, 19, diag1, 0)

    finish(b_copies)
    for j, x0, n, i0 in ((0, 1, 5, 3), (1, 6, 8, 0), (2, 14, 5, 0)):
        def spread_b(i, _, j=j, x0=x0, i0=i0):
            b = z_halo(LB[0, j], LB[1, j], B1[x0 + i], i + i0)
            B1[x0 + i] = b
            D1[x0 + i] = t_inv * I1[x0 + i] * b
            return 0

        lax.fori_loop(0, n, spread_b, 0)

    def residual(K, ref, b, x, xp, xm, low_y=None):
        v = ref[x]
        fy, fz = K[1, x], K[2, x]
        gz_ = fz * (v - shift(v, -1, 1))
        av = K[3, x] * v + K[0, x] * (v - ref[xp]) + K[0, xm] * (v - ref[xm])
        if low_y is None:
            gy_ = fy * (v - shift(v, -1, 0))
            av = av + (gy_ - shift(gy_, 1, 0))
        else:
            av = av + fy * (v - shift(v, -1, 0)) + low_y * (v - shift(v, 1, 0))
        av = av + (gz_ - shift(gz_, 1, 1))
        return v, b[x] - av

    def pre1(x, _):
        d, r = residual(K1, D1, B1, x, x + 1, x - 1)
        X1[x] = d + (ca * d + cb * I1[x] * r)
        return 0

    lax.fori_loop(2, 18, pre1, 0)

    r32 = iota((32, 128), 0)
    keep1 = ((r32 >= jnp.where(first[1], 8, 7)) & (r32 < jnp.where(last[1], 24, 25))
             & (lane32r >= jnp.where(first[2], 32, 31)) & (lane32r < jnp.where(last[2], 96, 97)))

    def res1(x, _):
        _, r = residual(K1, X1, B1, x, x + 1, x - 1)
        inside = ((x > 5) | jnp.logical_not(first[0])) & ((x < 14) | jnp.logical_not(last[0]))
        D1[x] = jnp.where(keep1 & inside, r, 0.0)
        return 0

    lax.fori_loop(5, 15, res1, 0)

    rows = []
    for i in range(4):
        x = 6 + 2 * i
        RX1[i] = 0.125 * (D1[x - 1] + D1[x + 2]) + 0.375 * (D1[x] + D1[x + 1])
        parts = [RX1[i, pl.ds(7 + k, 8, stride=2), :] for k in range(4)]
        rows.append(0.125 * (parts[0] + parts[3]) + 0.375 * (parts[1] + parts[2]))
    B2P[...] = packed(jnp.concatenate(rows, 0), restrict_weights(wi - 32, wo, in32))
    b2_copies = start(far_msgs(B2P, lambda g, j, ys: LB2.at[g, j, ys]), b2_s, b2_r)
    LB2[gx, 1, 8:16, :] = B2P[...]

    NX2 = 4 * GX
    finish(k2_copies)
    lane24 = iota((24, 128), 1)

    def unpack2(lm, lc, lp, i):
        return jnp.where(lane24 < 32, pltpu.roll(lm, 128 - 32 * i, 1),
                         jnp.where(lane24 < 64, pltpu.roll(lc, 160 - 32 * i, 1), pltpu.roll(lp, 192 - 32 * i, 1)))

    def spread_k2(x, _):
        g, i = x >> 2, x & 3
        for f in range(5):
            K2[f, x] = unpack2(LK2[g, 0, f], LK2[g, 1, f], LK2[g, 2, f], i)
        return 0

    lax.fori_loop(0, NX2, spread_k2, 0)

    def up(x):
        return lax.rem(x + 1, NX2)

    def down(x):
        return lax.rem(x + (NX2 - 1), NX2)

    def diag2(x, _):
        fz = K2[2, x]
        diag = (K2[3, x] + K2[0, x] + K2[0, down(x)]) + (K2[1, x] + K2[4, x]) + (fz + shift(fz, 1, 1))
        I2[x] = 1.0 / diag
        return 0

    lax.fori_loop(0, NX2, diag2, 0)

    t2_inv, factors2 = cheb_factors(6, 0.05, 2.0)
    finish(b2_copies)

    def spread_b2(x, _):
        g, i = x >> 2, x & 3
        b = unpack2(LB2[g, 0], LB2[g, 1], LB2[g, 2], i)
        Y2[x] = b
        d = t2_inv * I2[x] * b
        D2[x] = d
        X2[0, x] = d
        return 0

    lax.fori_loop(0, NX2, spread_b2, 0)

    r24 = iota((24, 128), 0)
    keep2 = ((r24 >= jnp.where(first[1], 8, 4)) & (r24 < jnp.where(last[1], 16, 20))
             & (lane24 >= jnp.where(first[2], 32, 24)) & (lane24 < jnp.where(last[2], 64, 72)))
    for n, (fa, fb) in enumerate(factors2):
        src, dst = X2.at[n % 2], X2.at[1 - n % 2]
        final = n == len(factors2) - 1

        def step(x, _, src=src, dst=dst, fa=fa, fb=fb, final=final):
            v, r = residual(K2, src, Y2, x, up(x), down(x), K2[4, x])
            d = fa * D2[x] + fb * I2[x] * r
            if final:
                dst[x] = jnp.where(keep2, v + d, 0.0)
            else:
                D2[x] = d
                dst[x] = v + d
            return 0

        lax.fori_loop(0, NX2, step, 0)
    x2 = X2.at[len(factors2) % 2]

    wp = prolong_weights(wi - 32, wo - 32)
    z1 = dot(x2[...].reshape(NX2 * 24, 128), wp).reshape(NX2, 24, 128)
    Y2[...] = z1

    def pro_y1(x, _):
        c = Y2[x]
        lower, upper = shift(c, 1, 0), shift(c, -1, 0)
        PY1[x, pl.ds(0, 16, stride=2), :] = (0.75 * c + 0.25 * lower)[4:20]
        PY1[x, pl.ds(1, 16, stride=2), :] = (0.75 * c + 0.25 * upper)[4:20]
        return 0

    lax.fori_loop(0, NX2, pro_y1, 0)

    def pro_x1(i, _):
        a = 4 * gx + (i - 3)

        def slab(k):
            return jnp.where((k >= 0) & (k < NX2), PY1[lax.rem(k + NX2, NX2)], 0.0)

        c = 0.75 * slab(a)
        X1[2 * i] = X1[2 * i] + (c + 0.25 * slab(a - 1))
        X1[2 * i + 1] = X1[2 * i + 1] + (c + 0.25 * slab(a + 1))
        return 0

    lax.fori_loop(1, 9, pro_x1, 0)

    def post1(x, _):
        v, r = residual(K1, X1, B1, x, x + 1, x - 1)
        d = t_inv * I1[x] * r
        D1[x] = d
        T1[x] = v + d
        return 0

    lax.fori_loop(3, 17, post1, 0)
    keep1p = ((r32 >= jnp.where(first[1], 8, 4)) & (r32 < jnp.where(last[1], 24, 28))
              & (lane32r >= jnp.where(first[2], 32, 28)) & (lane32r < jnp.where(last[2], 96, 100)))

    def post1b(x, _):
        v, r = residual(K1, T1, B1, x, x + 1, x - 1)
        inside = ((x > 5) | jnp.logical_not(first[0])) & ((x < 14) | jnp.logical_not(last[0]))
        X1[x] = jnp.where(keep1p & inside, v + (ca * D1[x] + cb * I1[x] * r), 0.0)
        return 0

    lax.fori_loop(4, 16, post1b, 0)

    pi, po = iota((128, 256), 0), iota((128, 256), 1)
    wq = prolong_weights(pi - 32, jnp.where(po < 192, po, po - 256))
    for i in range(12):
        z0 = dot(X1[4 + i], wq)
        lower, upper = shift(z0, 1, 0), shift(z0, -1, 0)
        ev, od = 0.75 * z0 + 0.25 * lower, 0.75 * z0 + 0.25 * upper
        for h in (0, 1):
            PY0[h, i, pl.ds(0, 24, stride=2), :] = ev[4:28, 128 * h:128 * h + 128]
            PY0[h, i, pl.ds(1, 24, stride=2), :] = od[4:28, 128 * h:128 * h + 128]

    def pro_x0(i, _):
        c = 0.75 * ld(PY0, i + 1)
        st(V, 2 * i, ld(V, 2 * i) + (c + 0.25 * ld(PY0, i)))
        st(V, 2 * i + 1, ld(V, 2 * i + 1) + (c + 0.25 * ld(PY0, i + 2)))
        return 0

    lax.fori_loop(0, 10, pro_x0, 0)

    def post0(x, _):
        v, r = residual0(V, x)
        d = t_inv * ld(ID, x) * r
        st(D, x, d)
        st(W, x, v + d)
        return 0

    lax.fori_loop(1, 19, post0, 0)

    def post0b(x, _):
        v, r = residual0(W, x)
        o = v + (ca * ld(D, x) + cb * ld(ID, x) * r)
        out[x - 2] = o[8:40, :128]
        return 0

    lax.fori_loop(2, 18, post0b, 0)


def solution(mesh):
    sizes = tuple(mesh.shape[a] for a in ("gx", "gy", "gz"))
    nfar = 9 * sizes[0] - 1
    nx2 = 4 * sizes[0]

    def vm(*shape):
        return pltpu.VMEM(shape, F32)

    dma = lambda n: pltpu.SemaphoreType.DMA((n,))
    scratch = [
        vm(5, 2, 20, 48, 128), vm(2, 20, 48, 128), vm(2, 20, 48, 128), vm(2, 20, 48, 128), vm(2, 20, 48, 128),
        vm(2, 8, 48, 128), vm(3, 32, 128), vm(2, 5, 48, 128), vm(1, 32, 128), vm(2, 3, 48, 128),
        vm(2, 20, 32, 128), vm(4, 20, 32, 128), vm(4, 16, 128), vm(2, 3, 4, 32, 128),
        vm(20, 32, 128), vm(20, 32, 128), vm(20, 32, 128), vm(20, 32, 128), vm(20, 32, 128),
        vm(16, 128), vm(2, 3, 32, 128), vm(4, 32, 128),
        vm(5, 8, 128), vm(sizes[0], 3, 5, 24, 128), vm(8, 128), vm(sizes[0], 3, 24, 128),
        vm(5, nx2, 24, 128), vm(nx2, 24, 128), vm(2, nx2, 24, 128), vm(nx2, 24, 128), vm(nx2, 24, 128),
        vm(nx2, 32, 128), vm(2, 12, 48, 128),
        dma(5), dma(29), dma(29), dma(26), dma(26), dma(26), dma(26), dma(26), dma(26),
        dma(nfar), dma(nfar), dma(nfar), dma(nfar),
    ]

    def local(right_side, face_x, face_y, face_z, absorb):
        return pl.pallas_call(
            functools.partial(kernel, sizes),
            out_shape=jax.ShapeDtypeStruct(right_side.shape, F32),
            in_specs=[pl.BlockSpec(memory_space=pl.ANY)] * 5,
            out_specs=pl.BlockSpec(memory_space=pltpu.VMEM),
            scratch_shapes=scratch,
            compiler_params=pltpu.CompilerParams(
                collective_id=0, has_side_effects=True, vmem_limit_bytes=40 * 1024 * 1024),
            name="vcycle",
        )(right_side, face_x, face_y, face_z, absorb)

    spec = P("gx", "gy", "gz")
    return jax.shard_map(local, mesh=mesh, in_specs=(spec,) * 5, out_specs=spec, check_vma=False)
```

profile of v0, /device:TPU:1, one launch (start us, length us, event | category | flops | bytes accessed | tf_op | source)
XLA Modules:
  0.0 94.2 jit_solution(17400824253185377585)
XLA Ops:
  0.0 0.0 copy-start
  0.0 0.9 %copy-done = f32[16,32,128]{2,1,0:T(8,128)S(1)} copy-done((f32[16,32,128]{2,1,0:T(8,128)S(1)}, f32[16,32,128]{2,1,0:T(8,128)}, u32[]{:S(2)}) %copy-start) | copy-done | bytes 262168
  1.0 0.0 copy-start.1
  1.0 0.9 %copy-done.1 = f32[16,32,128]{2,1,0:T(8,128)S(1)} copy-done((f32[16,32,128]{2,1,0:T(8,128)S(1)}, f32[16,32,128]{2,1,0:T(8,128)}, u32[]{:S(2)}) %copy-start.1) | copy-done | bytes 262168
  1.9 0.0 copy-start.2
  1.9 0.9 %copy-done.2 = f32[16,32,128]{2,1,0:T(8,128)S(1)} copy-done((f32[16,32,128]{2,1,0:T(8,128)S(1)}, f32[16,32,128]{2,1,0:T(8,128)}, u32[]{:S(2)}) %copy-start.2) | copy-done | bytes 262168
  2.9 0.0 copy-start.3
  2.9 0.9 %copy-done.3 = f32[16,32,128]{2,1,0:T(8,128)S(1)} copy-done((f32[16,32,128]{2,1,0:T(8,128)S(1)}, f32[16,32,128]{2,1,0:T(8,128)}, u32[]{:S(2)}) %copy-start.3) | copy-done | bytes 262168
  3.8 0.0 copy-start.4
  3.8 0.9 %copy-done.4 = f32[16,32,128]{2,1,0:T(8,128)S(1)} copy-done((f32[16,32,128]{2,1,0:T(8,128)S(1)}, f32[16,32,128]{2,1,0:T(8,128)}, u32[]{:S(2)}) %copy-start.4) | copy-done | bytes 262168
  4.8 88.7 %vcycle.1 = f32[16,32,128]{2,1,0:T(8,128)S(1)} custom-call(f32[16,32,128]{2,1,0:T(8,128)S(1)} %copy-done, f32[16,32,128]{2,1,0:T(8,128)S(1)} %copy-done.1, f32[16,32,128]{2,1,0:T(8,128)S(1)} %copy-done.2, f32[16,32,128]{2,1,0:T(8,128)S(1)} %copy-done.3, f32[16,32,128]{2,1,0:T(8,128)S(1)} %copy-done.4), custom_call_target="tpu_custom_call" | custom-call | tf_op jit(solution)/shard_map/vcycle/pallas_call | solution.py:598
  93.5 0.7 copy.7
Async XLA Ops:
  0.0 0.9 %copy-start = (f32[16,32,128]{2,1,0:T(8,128)S(1)}, f32[16,32,128]{2,1,0:T(8,128)}, u32[]{:S(2)}) copy-start(f32[16,32,128]{2,1,0:T(8,128)} %b_in.1) | copy-start | bytes 786436
  1.0 0.9 %copy-start.1 = (f32[16,32,128]{2,1,0:T(8,128)S(1)}, f32[16,32,128]{2,1,0:T(8,128)}, u32[]{:S(2)}) copy-start(f32[16,32,128]{2,1,0:T(8,128)} %fx_in.1) | copy-start | bytes 786436
  1.9 0.9 %copy-start.2 = (f32[16,32,128]{2,1,0:T(8,128)S(1)}, f32[16,32,128]{2,1,0:T(8,128)}, u32[]{:S(2)}) copy-start(f32[16,32,128]{2,1,0:T(8,128)} %fy_in.1) | copy-start | bytes 786436
  2.9 0.9 %copy-start.3 = (f32[16,32,128]{2,1,0:T(8,128)S(1)}, f32[16,32,128]{2,1,0:T(8,128)}, u32[]{:S(2)}) copy-start(f32[16,32,128]{2,1,0:T(8,128)} %fz_in.1) | copy-start | bytes 786436
  3.8 0.9 %copy-start.4 = (f32[16,32,128]{2,1,0:T(8,128)S(1)}, f32[16,32,128]{2,1,0:T(8,128)}, u32[]{:S(2)}) copy-start(f32[16,32,128]{2,1,0:T(8,128)} %s_in.1) | copy-start | bytes 786436
where the time goes:
time: 94.5 us; the launch traced here: 94.2 us
  Pallas kernels  88.7 us (94%)
  local copies, waits for them, and re-layouts  5.45 us (6%)
    pallas_call x1, Pallas kernels, local(): pl.pallas_call(functools.partial(kernel, sizes), out_shape=jax.ShapeDtype...  88.7 us
    unnamed x11, local copies, waits for them, and re-layouts  5.45 us

commit v1 on v0

--- a/solution.py
+++ b/solution.py
@@ -1,4 +1,5 @@
 import functools
+import math
 
 import jax
 import jax.numpy as jnp
@@ -32,6 +33,9 @@
     return 1.0 / centre, out
 
 
+EDGES = [(1, 1), (1, -1), (-1, 1), (-1, -1)]
+
+
 def iota(shape, dim):
     return lax.broadcasted_iota(jnp.int32, shape, dim)
 
@@ -56,11 +60,17 @@
     return jnp.where(coarse == k, 0.75, jnp.where(coarse == side, 0.25, 0.0))
 
 
+def loop(lo, hi, body, init=0):
+    for i in range(lo, hi):
+        init = body(i, init)
+    return init
+
+
 def kernel(sizes, b_in, fx_in, fy_in, fz_in, s_in, out,
            C, ID, V, D, W, RX, ZC, LC, ZV, LV,
            KP, K1, ZK, LK, B1, I1, X1, D1, T1, ZB, LB, RX1,
            K2P, LK2, B2P, LB2, K2, I2, X2, D2, Y2, PY1, PY0,
-           in_sem, c_s, c_r, v_s, v_r, k_s, k_r, b_s, b_r, k2_s, k2_r, b2_s, b2_r):
+           CY, CYL, CE, CEL, VY, VYL, VE, VEL, count, in_sem, sems):
     GX, GY, GZ = sizes
     gx, gy, gz = (lax.axis_index(a) for a in ("gx", "gy", "gz"))
     me = (gx, gy, gz)
@@ -80,21 +90,21 @@
     for d in far:
         pl.semaphore_signal(bar, inc=1, device_id=dev(d), device_id_type=MESH)
 
-    def start(msgs, ss, rs):
-        copies = []
-        for k, (d, src, dst) in enumerate(msgs):
+    def start(msgs, ss):
+        tiles = 0
+        for d, src, dst in msgs:
+            tiles += math.prod(dst.shape) // 1024
             c = pltpu.make_async_remote_copy(
-                src_ref=src, dst_ref=dst, send_sem=ss.at[k], recv_sem=rs.at[k],
+                src_ref=src, dst_ref=dst, send_sem=sems.at[ss], recv_sem=sems.at[ss + 1],
                 device_id=dev(d), device_id_type=MESH)
             c.start()
-            copies.append(c)
-        return copies
-
-    def finish(copies):
-        for c in copies:
-            c.wait_recv()
-        for c in copies:
-            c.wait_send()
+        return tiles, ss
+
+    def finish(sent):
+        tiles, ss = sent
+        span = count.at[pl.ds(0, tiles)]
+        pltpu.make_async_copy(span, span, sems.at[ss + 1]).wait()
+        pltpu.make_async_copy(span, span, sems.at[ss]).wait()
 
     lane128 = iota((1, 128), 1)
     first = [m == 0 for m in me]
@@ -112,7 +122,7 @@
         C[FZ, 0, x, 8:40, :] = jnp.where(last[2] & (lane32 == 127), 0.0, C[FZ, 0, x, 8:40, :])
         return 0
 
-    lax.fori_loop(2, 18, close, 0)
+    loop(2, 18, close, 0)
 
     TILES = ((0, 6), (6, 5), (11, 5))
 
@@ -123,33 +133,62 @@
                 v = pltpu.roll(C[f, 0, 2 + x0 + i, 8:40, :], 4 * g + 2, 1)
                 acc = jnp.where((lane32 >> 2) == g, v, acc)
             return acc
-        ZC[t] = lax.fori_loop(0, n, pack, jnp.zeros((32, 128), F32))
+        ZC[t] = loop(0, n, pack, jnp.zeros((32, 128), F32))
 
     pl.semaphore_wait(bar, len(far))
 
     ROWS = {1: (32, 0, 8), -1: (8, 40, 8), 0: (8, 8, 32)}
 
-    def fine_msgs(dirs, xs, field, zsrc, zland, ztiles):
+    def fine_msgs(xs, stack, ys, yland, zs, zland, es, eland, ztiles):
         msgs = []
-        for d in dirs:
+        for d in ALL26:
             dx, dy, dz = d
-            sy, ty, ny = ROWS[dy]
-            if dz == 0:
-                sx, tx, nx = xs[dx]
-                msgs.append((d, field(pl.ds(sx, nx), pl.ds(sy, ny)), field(pl.ds(tx, nx), pl.ds(ty, ny))))
-            else:
+            if dz != 0:
+                sy, ty, ny = ROWS[dy]
                 side = 0 if dz == 1 else 1
                 s0, t0, nt = ztiles[dx]
-                msgs.append((d, zsrc.at[pl.ds(s0, nt), pl.ds(sy - 8, ny)], zland.at[side, pl.ds(t0, nt), pl.ds(ty, ny)]))
+                msgs.append((d, zs.at[pl.ds(s0, nt), pl.ds(sy - 8, ny)], zland.at[side, pl.ds(t0, nt), pl.ds(ty, ny)]))
+            elif dy == 0:
+                sx, tx, nx = xs[dx]
+                msgs.append((d, stack(pl.ds(sx, nx)), stack(pl.ds(tx, nx))))
+            elif dx == 0:
+                side = 0 if dy == 1 else 1
+                msgs.append((d, ys.at[side], yland.at[side]))
+            else:
+                e = EDGES.index((dx, dy))
+                msgs.append((d, es.at[e], eland.at[e]))
         return msgs
 
-    cfield = lambda xs, ys: C.at[:, 0, xs, ys]
-    c_msgs = fine_msgs(ALL26, {1: (17, 1, 1), -1: (2, 18, 1), 0: (2, 2, 16)}, cfield, ZC, LC,
-                       {1: (2, 0, 1), 0: (0, 1, 3), -1: (0, 4, 1)})
-    for dy in (-1, 0, 1):
-        sy, ty, ny = ROWS[dy]
-        c_msgs.append(((1, dy, 0), C.at[FX, 0, pl.ds(16, 1), pl.ds(sy, ny)], C.at[FX, 0, pl.ds(0, 1), pl.ds(ty, ny)]))
-    c_copies = start(c_msgs, c_s, c_r)
+    CUP = [(f, 39, 7) for f in range(5)] + [(FY, 38, 6)]
+    CDOWN = [(f, 8, 40) for f in range(5)]
+    C2 = C.reshape(5 * 2 * 20 * 48, 128)
+
+    def crows(f, row):
+        return pl.ds((2 * f * 20 + 2) * 48 + row, 16, stride=48)
+
+    CY[1, 5] = jnp.zeros((16, 128), F32)
+    for side, rows in ((0, CUP), (1, CDOWN)):
+        for k, (f, here, _) in enumerate(rows):
+            CY[side, k] = C2[crows(f, here), :]
+
+    def cedge(dx, dy):
+        x, tx = (17, 1) if dx == 1 else (2, 18)
+        y, ty = (39, 7) if dy == 1 else (8, 40)
+        rows = [(f, x, y, tx, ty) for f in range(5)]
+        if dy == 1:
+            rows.append((FY, x, y - 1, tx, ty - 1))
+        if dx == 1:
+            rows.append((FX, x - 1, y, tx - 1, ty))
+        return rows
+
+    for e, (dx, dy) in enumerate(EDGES):
+        for k, (f, x, y, _, _) in enumerate(cedge(dx, dy)):
+            CE[e, k:k + 1, :] = C[f, 0, x, y:y + 1, :]
+
+    c_msgs = fine_msgs({1: (17, 1, 1), -1: (2, 18, 1)}, lambda xs: C.at[:, 0, xs, pl.ds(8, 32)],
+                       CY, CYL, ZC, LC, CE, CEL, {1: (2, 0, 1), 0: (0, 1, 3), -1: (0, 4, 1)})
+    c_msgs.append(((1, 0, 0), C.at[FX, 0, pl.ds(16, 1), pl.ds(8, 32)], C.at[FX, 0, pl.ds(0, 1), pl.ds(8, 32)]))
+    c_sent = start(c_msgs, 0)
 
     li, lo = iota((256, 128), 0), iota((256, 128), 1)
     hit = ((li & 127) >> 1) == (lo & 63)
@@ -171,7 +210,7 @@
         RX[1, i, 16:32, :] = ms
         return 0
 
-    lax.fori_loop(0, 8, mid, 0)
+    loop(0, 8, mid, 0)
     for p, w in ((0, wa), (1, wb)):
         lhs = jnp.concatenate(
             [RX[q, :, 16 * p:16 * p + 16, :].reshape(128, 128) for q in (0, 1)], axis=1)
@@ -205,12 +244,13 @@
                 msgs.append((d, zsrc(pl.ds(sy - 8, ny)), zland(side, 1 - dx, pl.ds(ty, ny))))
         return msgs
 
-    finish(c_copies)
-
-    k_copies = start(
-        mid_msgs({1: (8, 0, 6), -1: (6, 14, 5), 0: (6, 6, 8)},
-                 lambda xs, ys: KP.at[:, xs, ys],
-                 lambda ys: ZK.at[:, ys], lambda side, j, ys: LK.at[side, j, :, ys]), k_s, k_r)
+    finish(c_sent)
+    for side, rows in ((0, CUP), (1, CDOWN)):
+        for k, (f, _, there) in enumerate(rows):
+            C2[crows(f, there), :] = CYL[side, k]
+    for e, (dx, dy) in enumerate(EDGES):
+        for k, (f, _, _, x, y) in enumerate(cedge(dx, dy)):
+            C[f, 0, x, y:y + 1, :] = CEL[e, k:k + 1, :]
 
     lane48 = iota((48, 128), 1)
     for j, (x0, n, i0) in enumerate(((0, 2, 3), (2, 6, 0), (8, 5, 0), (13, 5, 0), (18, 2, 0))):
@@ -223,7 +263,7 @@
                 C[f, 1, x0 + i, :, :] = pltpu.roll(both, 126 + 128 - 4 * ((i + i0) * 5 + f), 1)
             return 0
 
-        lax.fori_loop(0, n, spread, 0)
+        loop(0, n, spread, 0)
 
     def ld(ref, x):
         return jnp.concatenate([ref[0, x], ref[1, x]], axis=1)
@@ -245,7 +285,7 @@
         st(D, x, t_inv * inv * ldc(B, x))
         return 0
 
-    lax.fori_loop(1, 19, diag0, 0)
+    loop(1, 19, diag0, 0)
 
     def residual0(ref, x):
         v = ld(ref, x)
@@ -261,16 +301,36 @@
         V[0, x, 8:40, :] = v[8:40, :128]
         return 0
 
-    lax.fori_loop(2, 18, pre0, 0)
+    loop(2, 18, pre0, 0)
 
     def pack_v(i, acc):
         v = pltpu.roll(V[0, 2 + i, 8:40, :], 4 * i + 2, 1)
         return jnp.where((lane32 >> 2) == i, v, acc)
 
-    ZV[0] = lax.fori_loop(0, 16, pack_v, jnp.zeros((32, 128), F32))
-    v_copies = start(
-        fine_msgs(ALL26, {1: (16, 0, 2), -1: (2, 18, 2), 0: (2, 2, 16)},
-                  lambda xs, ys: V.at[0, xs, ys], ZV, LV, {1: (0, 0, 1), 0: (0, 1, 1), -1: (0, 2, 1)}), v_s, v_r)
+    ZV[0] = loop(0, 16, pack_v, jnp.zeros((32, 128), F32))
+    V2 = V.reshape(2 * 20 * 48, 128)
+
+    def vrows(row):
+        return pl.ds(2 * 48 + row, 16, stride=48)
+
+    for k in (0, 1):
+        VY[0, k] = V2[vrows(38 + k), :]
+        VY[1, k] = V2[vrows(8 + k), :]
+
+    def vedge(dx, dy):
+        x, tx = (16, 0) if dx == 1 else (2, 18)
+        y, ty = (38, 6) if dy == 1 else (8, 40)
+        return [(x + a, y + b, tx + a, ty + b) for a in (0, 1) for b in (0, 1)]
+
+    for e, (dx, dy) in enumerate(EDGES):
+        for k, (x, y, _, _) in enumerate(vedge(dx, dy)):
+            VE[e, k:k + 1, :] = V[0, x, y:y + 1, :]
+    v_sent = start(fine_msgs({1: (16, 0, 2), -1: (2, 18, 2)}, lambda xs: V.at[0, xs, pl.ds(8, 32)],
+                             VY, VYL, ZV, LV, VE, VEL, {1: (0, 0, 1), 0: (0, 1, 1), -1: (0, 2, 1)}), 2)
+    k_sent = start(
+        mid_msgs({1: (8, 0, 6), -1: (6, 14, 5), 0: (6, 6, 8)},
+                 lambda xs, ys: KP.at[:, xs, ys],
+                 lambda ys: ZK.at[:, ys], lambda side, j, ys: LK.at[side, j, :, ys]), 4)
 
     wi, wo = iota((128, 128), 0), iota((128, 128), 1)
     in32 = wo < 32
@@ -304,10 +364,15 @@
     def far_msgs(src, land):
         return [(d, src, land(gx, 1 - d[2], pl.ds(8 - 8 * d[1], 8))) for d in far]
 
-    k2_copies = start(far_msgs(K2P, lambda g, j, ys: LK2.at[g, j, :, ys]), k2_s, k2_r)
     LK2[gx, 1, :, 8:16, :] = K2P[...]
 
-    finish(v_copies)
+    finish(v_sent)
+    for k in (0, 1):
+        V2[vrows(6 + k), :] = VYL[0, k]
+        V2[vrows(40 + k), :] = VYL[1, k]
+    for e, (dx, dy) in enumerate(EDGES):
+        for k, (_, _, x, y) in enumerate(vedge(dx, dy)):
+            V[0, x, y:y + 1, :] = VEL[e, k:k + 1, :]
     for j, (x0, n, i0) in enumerate(((0, 2, 14), (2, 16, 0), (18, 2, 0))):
         LV[0, j] = jnp.where((lane48 & 3) >= 2, LV[1, j], LV[0, j])
 
@@ -315,7 +380,7 @@
             V[1, x0 + i, :, :] = pltpu.roll(LV[0, j], 126 + 128 - 4 * (i + i0), 1)
             return 0
 
-        lax.fori_loop(0, n, spread_v, 0)
+        loop(0, n, spread_v, 0)
 
     r48, l256 = iota((48, 256), 0), iota((48, 256), 1)
     keep0 = ((r48 >= jnp.where(first[1], 8, 7)) & (r48 < jnp.where(last[1], 40, 41))
@@ -327,7 +392,7 @@
         st(D, x, jnp.where(keep0 & inside, r, 0.0))
         return 0
 
-    lax.fori_loop(1, 19, res0, 0)
+    loop(1, 19, res0, 0)
 
     def rest0(i, _):
         x = 2 + 2 * i
@@ -338,18 +403,20 @@
             RX[h, i, 0:16, :] = 0.125 * (rows[0] + rows[3]) + 0.375 * (rows[1] + rows[2])
         return 0
 
-    lax.fori_loop(0, 8, rest0, 0)
+    loop(0, 8, rest0, 0)
     zin = jnp.where(li < 192, li, li - 256)
     wr = restrict_weights(zin, lo - 32, (lo >= 32) & (lo < 96))
     lhs = jnp.concatenate([RX[h, :, 0:16, :].reshape(128, 128) for h in (0, 1)], axis=1)
     B1[6:14, 8:24, :] = dot(lhs, wr).reshape(8, 16, 128)
     ZB[...] = pack_mid(lambda x: B1[6 + x, 8:24, :], 32)
-    b_copies = start(
+    b_sent = start(
         mid_msgs({1: (9, 1, 5), -1: (6, 14, 5), 0: (6, 6, 8)},
                  lambda xs, ys: B1.at[xs, ys],
-                 lambda ys: ZB.at[ys], lambda side, j, ys: LB.at[side, j, ys]), b_s, b_r)
-
-    finish(k_copies)
+                 lambda ys: ZB.at[ys], lambda side, j, ys: LB.at[side, j, ys]), 6)
+
+    k2_sent = start(far_msgs(K2P, lambda g, j, ys: LK2.at[g, j, :, ys]), 8)
+
+    finish(k_sent)
     lane32r = iota((32, 128), 1)
 
     def z_halo(lm, lp, own, q):
@@ -365,7 +432,7 @@
                 K1[f, x0 + i] = z_halo(LK[0, j, f], LK[1, j, f], own, i + i0)
             return 0
 
-        lax.fori_loop(0, n, spread_k, 0)
+        loop(0, n, spread_k, 0)
 
     def diag1(x, _):
         fy, fz = K1[1, x], K1[2, x]
@@ -373,9 +440,9 @@
         I1[x] = 1.0 / diag
         return 0
 
-    lax.fori_loop(1, 19, diag1, 0)
-
-    finish(b_copies)
+    loop(1, 19, diag1, 0)
+
+    finish(b_sent)
     for j, x0, n, i0 in ((0, 1, 5, 3), (1, 6, 8, 0), (2, 14, 5, 0)):
         def spread_b(i, _, j=j, x0=x0, i0=i0):
             b = z_halo(LB[0, j], LB[1, j], B1[x0 + i], i + i0)
@@ -383,7 +450,7 @@
             D1[x0 + i] = t_inv * I1[x0 + i] * b
             return 0
 
-        lax.fori_loop(0, n, spread_b, 0)
+        loop(0, n, spread_b, 0)
 
     def residual(K, ref, b, x, xp, xm, low_y=None):
         v = ref[x]
@@ -403,7 +470,7 @@
         X1[x] = d + (ca * d + cb * I1[x] * r)
         return 0
 
-    lax.fori_loop(2, 18, pre1, 0)
+    loop(2, 18, pre1, 0)
 
     r32 = iota((32, 128), 0)
     keep1 = ((r32 >= jnp.where(first[1], 8, 7)) & (r32 < jnp.where(last[1], 24, 25))
@@ -415,7 +482,7 @@
         D1[x] = jnp.where(keep1 & inside, r, 0.0)
         return 0
 
-    lax.fori_loop(5, 15, res1, 0)
+    loop(5, 15, res1, 0)
 
     rows = []
     for i in range(4):
@@ -424,11 +491,11 @@
         parts = [RX1[i, pl.ds(7 + k, 8, stride=2), :] for k in range(4)]
         rows.append(0.125 * (parts[0] + parts[3]) + 0.375 * (parts[1] + parts[2]))
     B2P[...] = packed(jnp.concatenate(rows, 0), restrict_weights(wi - 32, wo, in32))
-    b2_copies = start(far_msgs(B2P, lambda g, j, ys: LB2.at[g, j, ys]), b2_s, b2_r)
+    b2_sent = start(far_msgs(B2P, lambda g, j, ys: LB2.at[g, j, ys]), 10)
     LB2[gx, 1, 8:16, :] = B2P[...]
 
     NX2 = 4 * GX
-    finish(k2_copies)
+    finish(k2_sent)
     lane24 = iota((24, 128), 1)
 
     def unpack2(lm, lc, lp, i):
@@ -441,7 +508,7 @@
             K2[f, x] = unpack2(LK2[g, 0, f], LK2[g, 1, f], LK2[g, 2, f], i)
         return 0
 
-    lax.fori_loop(0, NX2, spread_k2, 0)
+    loop(0, NX2, spread_k2, 0)
 
     def up(x):
         return lax.rem(x + 1, NX2)
@@ -455,10 +522,10 @@
         I2[x] = 1.0 / diag
         return 0
 
-    lax.fori_loop(0, NX2, diag2, 0)
+    loop(0, NX2, diag2, 0)
 
     t2_inv, factors2 = cheb_factors(6, 0.05, 2.0)
-    finish(b2_copies)
+    finish(b2_sent)
 
     def spread_b2(x, _):
         g, i = x >> 2, x & 3
@@ -469,7 +536,7 @@
         X2[0, x] = d
         return 0
 
-    lax.fori_loop(0, NX2, spread_b2, 0)
+    loop(0, NX2, spread_b2, 0)
 
     r24 = iota((24, 128), 0)
     keep2 = ((r24 >= jnp.where(first[1], 8, 4)) & (r24 < jnp.where(last[1], 16, 20))
@@ -488,7 +555,7 @@
                 dst[x] = v + d
             return 0
 
-        lax.fori_loop(0, NX2, step, 0)
+        loop(0, NX2, step, 0)
     x2 = X2.at[len(factors2) % 2]
 
     wp = prolong_weights(wi - 32, wo - 32)
@@ -502,7 +569,7 @@
         PY1[x, pl.ds(1, 16, stride=2), :] = (0.75 * c + 0.25 * upper)[4:20]
         return 0
 
-    lax.fori_loop(0, NX2, pro_y1, 0)
+    loop(0, NX2, pro_y1, 0)
 
     def pro_x1(i, _):
         a = 4 * gx + (i - 3)
@@ -515,7 +582,7 @@
         X1[2 * i + 1] = X1[2 * i + 1] + (c + 0.25 * slab(a + 1))
         return 0
 
-    lax.fori_loop(1, 9, pro_x1, 0)
+    loop(1, 9, pro_x1, 0)
 
     def post1(x, _):
         v, r = residual(K1, X1, B1, x, x + 1, x - 1)
@@ -524,7 +591,7 @@
         T1[x] = v + d
         return 0
 
-    lax.fori_loop(3, 17, post1, 0)
+    loop(3, 17, post1, 0)
     keep1p = ((r32 >= jnp.where(first[1], 8, 4)) & (r32 < jnp.where(last[1], 24, 28))
               & (lane32r >= jnp.where(first[2], 32, 28)) & (lane32r < jnp.where(last[2], 96, 100)))
 
@@ -534,7 +601,7 @@
         X1[x] = jnp.where(keep1p & inside, v + (ca * D1[x] + cb * I1[x] * r), 0.0)
         return 0
 
-    lax.fori_loop(4, 16, post1b, 0)
+    loop(4, 16, post1b, 0)
 
     pi, po = iota((128, 256), 0), iota((128, 256), 1)
     wq = prolong_weights(pi - 32, jnp.where(po < 192, po, po - 256))
@@ -552,7 +619,7 @@
         st(V, 2 * i + 1, ld(V, 2 * i + 1) + (c + 0.25 * ld(PY0, i + 2)))
         return 0
 
-    lax.fori_loop(0, 10, pro_x0, 0)
+    loop(0, 10, pro_x0, 0)
 
     def post0(x, _):
         v, r = residual0(V, x)
@@ -561,7 +628,7 @@
         st(W, x, v + d)
         return 0
 
-    lax.fori_loop(1, 19, post0, 0)
+    loop(1, 19, post0, 0)
 
     def post0b(x, _):
         v, r = residual0(W, x)
@@ -569,12 +636,11 @@
         out[x - 2] = o[8:40, :128]
         return 0
 
-    lax.fori_loop(2, 18, post0b, 0)
+    loop(2, 18, post0b, 0)
 
 
 def solution(mesh):
     sizes = tuple(mesh.shape[a] for a in ("gx", "gy", "gz"))
-    nfar = 9 * sizes[0] - 1
     nx2 = 4 * sizes[0]
 
     def vm(*shape):
@@ -590,19 +656,20 @@
         vm(5, 8, 128), vm(sizes[0], 3, 5, 24, 128), vm(8, 128), vm(sizes[0], 3, 24, 128),
         vm(5, nx2, 24, 128), vm(nx2, 24, 128), vm(2, nx2, 24, 128), vm(nx2, 24, 128), vm(nx2, 24, 128),
         vm(nx2, 32, 128), vm(2, 12, 48, 128),
-        dma(5), dma(29), dma(29), dma(26), dma(26), dma(26), dma(26), dma(26), dma(26),
-        dma(nfar), dma(nfar), dma(nfar), dma(nfar),
+        vm(2, 6, 16, 128), vm(2, 6, 16, 128), vm(4, 8, 128), vm(4, 8, 128),
+        vm(2, 2, 16, 128), vm(2, 2, 16, 128), vm(4, 8, 128), vm(4, 8, 128),
+        vm(512, 8, 128), dma(5), dma(12),
     ]
 
     def local(right_side, face_x, face_y, face_z, absorb):
         return pl.pallas_call(
             functools.partial(kernel, sizes),
             out_shape=jax.ShapeDtypeStruct(right_side.shape, F32),
-            in_specs=[pl.BlockSpec(memory_space=pl.ANY)] * 5,
+            in_specs=[pl.BlockSpec(memory_space=pltpu.HBM)] * 5,
             out_specs=pl.BlockSpec(memory_space=pltpu.VMEM),
             scratch_shapes=scratch,
             compiler_params=pltpu.CompilerParams(
-                collective_id=0, has_side_effects=True, vmem_limit_bytes=40 * 1024 * 1024),
+                collective_id=0, has_side_effects=True, vmem_limit_bytes=62 * 1024 * 1024),
             name="vcycle",
         )(right_side, face_x, face_y, face_z, absorb)
 

time: 94.5 us -> 54.3 us (0.57)
  Pallas kernels: 88.7 us -> 52.5 us
  local copies, waits for them, and re-layouts: 5.45 us -> 1.67 us
    pallas_call x1, Pallas kernels: 88.7 us -> 52.5 us  [local(): pl.pallas_call(functools.partial(kernel, sizes), out_shape=jax.ShapeDtype...]
    unnamed x11 -> x1, local copies, waits for them, and re-layouts: 5.45 us -> 1.67 us
where the time goes in v1:
time: 54.3 us; the launch traced here: 54.2 us
  Pallas kernels  52.5 us (97%)
  local copies, waits for them, and re-layouts  1.67 us (3%)
    pallas_call x1, Pallas kernels, local(): pl.pallas_call(functools.partial(kernel, sizes), out_shape=jax.ShapeDtype...  52.5 us
    unnamed x1, local copies, waits for them, and re-layouts  1.67 us

profile of v1, /device:TPU:1, one launch (start us, length us, event | category | flops | bytes accessed | tf_op | source)
XLA Modules:
  0.0 54.2 jit_solution(14126861369789568892)
XLA Ops:
  0.0 52.5 %vcycle.1 = f32[16,32,128]{2,1,0:T(8,128)} custom-call(f32[16,32,128]{2,1,0:T(8,128)} %b_in.1, f32[16,32,128]{2,1,0:T(8,128)} %fx_in.1, f32[16,32,128]{2,1,0:T(8,128)} %fy_in.1, f32[16,32,128]{2,1,0:T(8,128)} %fz_in.1, f32[16,32,128]{2,1,0:T(8,128)} %s_in.1), custom_call_target="tpu_custom_call" | custom-call | tf_op jit(solution)/shard_map/vcycle/pallas_call | solution.py:665
  52.5 1.7 %copy.7 = f32[16,32,128]{2,1,0:T(8,128)} copy(f32[16,32,128]{2,1,0:T(8,128)} %vcycle.1) | data formatting | bytes 524288

commit v2 on v1

--- a/solution.py
+++ b/solution.py
@@ -295,10 +295,22 @@
         av = av + (gy_ - shift(gy_, 1, 0)) + (gz_ - shift(gz_, 1, 1))
         return v, ldc(B, x) - av
 
+    def own_residual0(ref, x):
+        wide, fy = ref[0, x], C[FY, 0, x]
+        flux = fy * (wide - shift(wide, -1, 0))
+        av = (flux - shift(flux, 1, 0))[8:40]
+        v, side = wide[8:40], ref[1, x, 8:40, :]
+        fz = C[FZ, 0, x, 8:40, :]
+        low_z = shift(jnp.where(lane32 == 127, C[FZ, 1, x, 8:40, :], fz), 1, 1)
+        av = av + fz * (v - shift(jnp.where(lane32 == 0, side, v), -1, 1))
+        av = av + low_z * (v - shift(jnp.where(lane32 == 127, side, v), 1, 1))
+        av = av + C[FX, 0, x, 8:40, :] * (v - ref[0, x + 1, 8:40, :])
+        av = av + C[FX, 0, x - 1, 8:40, :] * (v - ref[0, x - 1, 8:40, :])
+        return v, C[B, 0, x, 8:40, :] - (av + C[S, 0, x, 8:40, :] * v)
+
     def pre0(x, _):
-        d, r = residual0(D, x)
-        v = d + (ca * d + cb * ld(ID, x) * r)
-        V[0, x, 8:40, :] = v[8:40, :128]
+        d, r = own_residual0(D, x)
+        V[0, x, 8:40, :] = d + (ca * d + cb * ID[0, x, 8:40, :] * r)
         return 0
 
     loop(2, 18, pre0, 0)
@@ -631,9 +643,8 @@
     loop(1, 19, post0, 0)
 
     def post0b(x, _):
-        v, r = residual0(W, x)
-        o = v + (ca * ld(D, x) + cb * ld(ID, x) * r)
-        out[x - 2] = o[8:40, :128]
+        v, r = own_residual0(W, x)
+        out[x - 2] = v + (ca * D[0, x, 8:40, :] + cb * ID[0, x, 8:40, :] * r)
         return 0
 
     loop(2, 18, post0b, 0)

time: 54.3 us -> 54.3 us (level)
  no operation moved by 1% of the time
where the time goes in v2:
time: 54.3 us; the launch traced here: 54.1 us
  Pallas kernels  52.5 us (97%)
  local copies, waits for them, and re-layouts  1.67 us (3%)
    pallas_call x1, Pallas kernels, local(): pl.pallas_call(functools.partial(kernel, sizes), out_shape=jax.ShapeDtype...  52.5 us
    unnamed x1, local copies, waits for them, and re-layouts  1.67 us

profile of v2, /device:TPU:1, one launch (start us, length us, event | category | flops | bytes accessed | tf_op | source)
XLA Modules:
  0.0 54.1 jit_solution(15875080876562650427)
XLA Ops:
  0.0 52.5 %vcycle.1 = f32[16,32,128]{2,1,0:T(8,128)} custom-call(f32[16,32,128]{2,1,0:T(8,128)} %b_in.1, f32[16,32,128]{2,1,0:T(8,128)} %fx_in.1, f32[16,32,128]{2,1,0:T(8,128)} %fy_in.1, f32[16,32,128]{2,1,0:T(8,128)} %fz_in.1, f32[16,32,128]{2,1,0:T(8,128)} %s_in.1), custom_call_target="tpu_custom_call" | custom-call | tf_op jit(solution)/shard_map/vcycle/pallas_call | solution.py:676
  52.5 1.7 %copy.7 = f32[16,32,128]{2,1,0:T(8,128)} copy(f32[16,32,128]{2,1,0:T(8,128)} %vcycle.1) | data formatting | bytes 524288

commit v3 on v2

--- a/solution.py
+++ b/solution.py
@@ -60,10 +60,19 @@
     return jnp.where(coarse == k, 0.75, jnp.where(coarse == side, 0.25, 0.0))
 
 
-def loop(lo, hi, body, init=0):
-    for i in range(lo, hi):
-        init = body(i, init)
-    return init
+def loop(lo, hi, body, init=0, chunks=1):
+    u = (hi - lo) // chunks
+    if chunks == 1:
+        for i in range(lo, hi):
+            init = body(i, init)
+        return init
+
+    def chunk(c, carry):
+        for k in range(u):
+            carry = body(lo + c * u + k, carry)
+        return carry
+
+    return lax.fori_loop(0, chunks, chunk, init)
 
 
 def kernel(sizes, b_in, fx_in, fy_in, fz_in, s_in, out,
@@ -226,8 +235,14 @@
             acc = jnp.where((lane16 >> 3) == 2 * x + 1, shift(v, 16 * x + 8 - base, 1), acc)
         return acc
 
-    for f in range(4):
-        ZK[f] = pack_mid(lambda x: KP[f // 2, 6 + x, 8:24, :], 64 * (f % 2))
+    for t in range(2):
+        acc = [jnp.zeros((16, 128), F32)] * 2
+        for x in range(8):
+            for side, edge in ((0, 56), (1, 0)):
+                v = shift(KP[t, 6 + x, 8:24, :], 8 * x - edge, 1)
+                acc[side] = jnp.where(((lane16 >> 3) & 7) == x, v, acc[side])
+        ZK[0, t] = acc[0]
+        ZK[1, t] = acc[1]
 
     MROWS = {1: (16, 0, 8), -1: (8, 24, 8), 0: (8, 8, 16)}
 
@@ -241,7 +256,7 @@
                 msgs.append((d, field(pl.ds(sx, nx), pl.ds(sy, ny)), field(pl.ds(tx, nx), pl.ds(ty, ny))))
             else:
                 side = 0 if dz == 1 else 1
-                msgs.append((d, zsrc(pl.ds(sy - 8, ny)), zland(side, 1 - dx, pl.ds(ty, ny))))
+                msgs.append((d, zsrc(side, pl.ds(sy - 8, ny)), zland(side, 1 - dx, pl.ds(ty, ny))))
         return msgs
 
     finish(c_sent)
@@ -285,7 +300,7 @@
         st(D, x, t_inv * inv * ldc(B, x))
         return 0
 
-    loop(1, 19, diag0, 0)
+    loop(1, 19, diag0, 0, chunks=2)
 
     def residual0(ref, x):
         v = ld(ref, x)
@@ -313,7 +328,7 @@
         V[0, x, 8:40, :] = d + (ca * d + cb * ID[0, x, 8:40, :] * r)
         return 0
 
-    loop(2, 18, pre0, 0)
+    loop(2, 18, pre0, 0, chunks=2)
 
     def pack_v(i, acc):
         v = pltpu.roll(V[0, 2 + i, 8:40, :], 4 * i + 2, 1)
@@ -342,7 +357,7 @@
     k_sent = start(
         mid_msgs({1: (8, 0, 6), -1: (6, 14, 5), 0: (6, 6, 8)},
                  lambda xs, ys: KP.at[:, xs, ys],
-                 lambda ys: ZK.at[:, ys], lambda side, j, ys: LK.at[side, j, :, ys]), 4)
+                 lambda side, ys: ZK.at[side, :, ys], lambda side, j, ys: LK.at[side, j, :, ys]), 4)
 
     wi, wo = iota((128, 128), 0), iota((128, 128), 1)
     in32 = wo < 32
@@ -373,8 +388,11 @@
     below = packed(rim, jnp.where(((wi >> 2) == wo) & in32, 1.0 / 256, 0.0))
     K2P[4] = jnp.where(row8 == 0, below, shift(K2P[1], 1, 0))
 
+    def nk(d):
+        return 5 if d[1] == 1 else 4
+
     def far_msgs(src, land):
-        return [(d, src, land(gx, 1 - d[2], pl.ds(8 - 8 * d[1], 8))) for d in far]
+        return [(d, src(d), land(d, gx, 1 - d[2], pl.ds(8 - 8 * d[1], 8))) for d in far]
 
     LK2[gx, 1, :, 8:16, :] = K2P[...]
 
@@ -404,7 +422,7 @@
         st(D, x, jnp.where(keep0 & inside, r, 0.0))
         return 0
 
-    loop(1, 19, res0, 0)
+    loop(1, 19, res0, 0, chunks=2)
 
     def rest0(i, _):
         x = 2 + 2 * i
@@ -424,9 +442,9 @@
     b_sent = start(
         mid_msgs({1: (9, 1, 5), -1: (6, 14, 5), 0: (6, 6, 8)},
                  lambda xs, ys: B1.at[xs, ys],
-                 lambda ys: ZB.at[ys], lambda side, j, ys: LB.at[side, j, ys]), 6)
-
-    k2_sent = start(far_msgs(K2P, lambda g, j, ys: LK2.at[g, j, :, ys]), 8)
+                 lambda side, ys: ZB.at[ys], lambda side, j, ys: LB.at[side, j, ys]), 6)
+
+    k2_sent = start(far_msgs(lambda d: K2P.at[pl.ds(0, nk(d))], lambda d, g, j, ys: LK2.at[g, j, pl.ds(0, nk(d)), ys]), 8)
 
     finish(k_sent)
     lane32r = iota((32, 128), 1)
@@ -441,7 +459,9 @@
         def spread_k(i, _, j=j, x0=x0, i0=i0):
             for f in range(4):
                 own = pltpu.roll(KP[f // 2, x0 + i], 32 if f % 2 == 0 else 96, 1)
-                K1[f, x0 + i] = z_halo(LK[0, j, f], LK[1, j, f], own, i + i0)
+                at = 8 * (i + i0) + 64 * (f % 2)
+                low, high = shift(LK[0, j, f // 2], 24 - at, 1), shift(LK[1, j, f // 2], 96 - at, 1)
+                K1[f, x0 + i] = jnp.where(lane32r < 32, low, jnp.where(lane32r < 96, own, high))
             return 0
 
         loop(0, n, spread_k, 0)
@@ -503,7 +523,7 @@
         parts = [RX1[i, pl.ds(7 + k, 8, stride=2), :] for k in range(4)]
         rows.append(0.125 * (parts[0] + parts[3]) + 0.375 * (parts[1] + parts[2]))
     B2P[...] = packed(jnp.concatenate(rows, 0), restrict_weights(wi - 32, wo, in32))
-    b2_sent = start(far_msgs(B2P, lambda g, j, ys: LB2.at[g, j, ys]), 10)
+    b2_sent = start(far_msgs(lambda d: B2P, lambda d, g, j, ys: LB2.at[g, j, ys]), 10)
     LB2[gx, 1, 8:16, :] = B2P[...]
 
     NX2 = 4 * GX
@@ -516,8 +536,10 @@
 
     def spread_k2(x, _):
         g, i = x >> 2, x & 3
-        for f in range(5):
-            K2[f, x] = unpack2(LK2[g, 0, f], LK2[g, 1, f], LK2[g, 2, f], i)
+        k2 = [unpack2(LK2[g, 0, f], LK2[g, 1, f], LK2[g, 2, f], i) for f in range(5)]
+        for f in range(4):
+            K2[f, x] = k2[f]
+        K2[4, x] = jnp.where(iota((24, 128), 0) < 8, k2[4], shift(k2[1], 1, 0))
         return 0
 
     loop(0, NX2, spread_k2, 0)
@@ -640,14 +662,14 @@
         st(W, x, v + d)
         return 0
 
-    loop(1, 19, post0, 0)
+    loop(1, 19, post0, 0, chunks=2)
 
     def post0b(x, _):
         v, r = own_residual0(W, x)
         out[x - 2] = v + (ca * D[0, x, 8:40, :] + cb * ID[0, x, 8:40, :] * r)
         return 0
 
-    loop(2, 18, post0b, 0)
+    loop(2, 18, post0b, 0, chunks=2)
 
 
 def solution(mesh):
@@ -661,7 +683,7 @@
     scratch = [
         vm(5, 2, 20, 48, 128), vm(2, 20, 48, 128), vm(2, 20, 48, 128), vm(2, 20, 48, 128), vm(2, 20, 48, 128),
         vm(2, 8, 48, 128), vm(3, 32, 128), vm(2, 5, 48, 128), vm(1, 32, 128), vm(2, 3, 48, 128),
-        vm(2, 20, 32, 128), vm(4, 20, 32, 128), vm(4, 16, 128), vm(2, 3, 4, 32, 128),
+        vm(2, 20, 32, 128), vm(4, 20, 32, 128), vm(2, 2, 16, 128), vm(2, 3, 2, 32, 128),
         vm(20, 32, 128), vm(20, 32, 128), vm(20, 32, 128), vm(20, 32, 128), vm(20, 32, 128),
         vm(16, 128), vm(2, 3, 32, 128), vm(4, 32, 128),
         vm(5, 8, 128), vm(sizes[0], 3, 5, 24, 128), vm(8, 128), vm(sizes[0], 3, 24, 128),

time: 54.3 us -> 53.5 us (0.985)
  Pallas kernels: 52.5 us -> 51.6 us
    pallas_call x1, Pallas kernels: 52.5 us -> 51.6 us  [local(): pl.pallas_call(functools.partial(kernel, sizes), out_shape=jax.ShapeDtype...]
where the time goes in v3:
time: 53.5 us; the launch traced here: 53.3 us
  Pallas kernels  51.6 us (96%)
  local copies, waits for them, and re-layouts  1.67 us (3%)
    pallas_call x1, Pallas kernels, local(): pl.pallas_call(functools.partial(kernel, sizes), out_shape=jax.ShapeDtype...  51.6 us
    unnamed x1, local copies, waits for them, and re-layouts  1.67 us

profile of v3, /device:TPU:1, one launch (start us, length us, event | category | flops | bytes accessed | tf_op | source)
XLA Modules:
  0.0 53.3 jit_solution(13607108374738960333)
XLA Ops:
  0.0 51.6 %vcycle.1 = f32[16,32,128]{2,1,0:T(8,128)} custom-call(f32[16,32,128]{2,1,0:T(8,128)} %b_in.1, f32[16,32,128]{2,1,0:T(8,128)} %fx_in.1, f32[16,32,128]{2,1,0:T(8,128)} %fy_in.1, f32[16,32,128]{2,1,0:T(8,128)} %fz_in.1, f32[16,32,128]{2,1,0:T(8,128)} %s_in.1), custom_call_target="tpu_custom_call" | custom-call | tf_op jit(solution)/shard_map/vcycle/pallas_call | solution.py:698
  51.6 1.7 %copy.7 = f32[16,32,128]{2,1,0:T(8,128)} copy(f32[16,32,128]{2,1,0:T(8,128)} %vcycle.1) | data formatting | bytes 524288

commit v4 on v3

--- a/solution.py
+++ b/solution.py
@@ -78,7 +78,7 @@
 def kernel(sizes, b_in, fx_in, fy_in, fz_in, s_in, out,
            C, ID, V, D, W, RX, ZC, LC, ZV, LV,
            KP, K1, ZK, LK, B1, I1, X1, D1, T1, ZB, LB, RX1,
-           K2P, LK2, B2P, LB2, K2, I2, X2, D2, Y2, PY1, PY0,
+           K2P, LK2, K2Z, LK2Z, B2P, LB2, K2, I2, X2, D2, Y2, PY1, PY0,
            CY, CYL, CE, CEL, VY, VYL, VE, VEL, count, in_sem, sems):
     GX, GY, GZ = sizes
     gx, gy, gz = (lax.axis_index(a) for a in ("gx", "gy", "gz"))
@@ -394,7 +394,23 @@
     def far_msgs(src, land):
         return [(d, src(d), land(d, gx, 1 - d[2], pl.ds(8 - 8 * d[1], 8))) for d in far]
 
-    LK2[gx, 1, :, 8:16, :] = K2P[...]
+    LK2[gx, :, 8:16, :] = K2P[...]
+
+    lane8 = iota((8, 128), 1)
+
+    def spot(f, i):
+        g = 4 * f + i
+        return g // 10, 12 * (g % 10)
+
+    for side, edge in ((0, 20), (1, 0)):
+        acc = [jnp.zeros((8, 128), F32)] * 2
+        for f in range(5):
+            for i in range(4):
+                t, at = spot(f, i)
+                v = shift(K2P[f], at - 32 * i - edge, 1)
+                acc[t] = jnp.where((lane8 >= at) & (lane8 < at + 12), v, acc[t])
+        K2Z[side, 0] = acc[0]
+        K2Z[side, 1] = acc[1]
 
     finish(v_sent)
     for k in (0, 1):
@@ -444,7 +460,9 @@
                  lambda xs, ys: B1.at[xs, ys],
                  lambda side, ys: ZB.at[ys], lambda side, j, ys: LB.at[side, j, ys]), 6)
 
-    k2_sent = start(far_msgs(lambda d: K2P.at[pl.ds(0, nk(d))], lambda d, g, j, ys: LK2.at[g, j, pl.ds(0, nk(d)), ys]), 8)
+    k2_sent = start(far_msgs(
+        lambda d: K2P.at[pl.ds(0, nk(d))] if d[2] == 0 else K2Z.at[(1 - d[2]) // 2],
+        lambda d, g, j, ys: LK2.at[g, pl.ds(0, nk(d)), ys] if d[2] == 0 else LK2Z.at[g, j // 2, :, ys]), 8)
 
     finish(k_sent)
     lane32r = iota((32, 128), 1)
@@ -536,7 +554,12 @@
 
     def spread_k2(x, _):
         g, i = x >> 2, x & 3
-        k2 = [unpack2(LK2[g, 0, f], LK2[g, 1, f], LK2[g, 2, f], i) for f in range(5)]
+        k2 = []
+        for f in range(5):
+            t, at = spot(f, i)
+            low, high = shift(LK2Z[g, 0, t], 20 - at, 1), shift(LK2Z[g, 1, t], 64 - at, 1)
+            own = shift(LK2[g, f], 32 - 32 * i, 1)
+            k2.append(jnp.where(lane24 < 32, low, jnp.where(lane24 < 64, own, high)))
         for f in range(4):
             K2[f, x] = k2[f]
         K2[4, x] = jnp.where(iota((24, 128), 0) < 8, k2[4], shift(k2[1], 1, 0))
@@ -574,7 +597,7 @@
 
     r24 = iota((24, 128), 0)
     keep2 = ((r24 >= jnp.where(first[1], 8, 4)) & (r24 < jnp.where(last[1], 16, 20))
-             & (lane24 >= jnp.where(first[2], 32, 24)) & (lane24 < jnp.where(last[2], 64, 72)))
+             & (lane24 >= jnp.where(first[2], 32, 28)) & (lane24 < jnp.where(last[2], 64, 68)))
     for n, (fa, fb) in enumerate(factors2):
         src, dst = X2.at[n % 2], X2.at[1 - n % 2]
         final = n == len(factors2) - 1
@@ -686,7 +709,8 @@
         vm(2, 20, 32, 128), vm(4, 20, 32, 128), vm(2, 2, 16, 128), vm(2, 3, 2, 32, 128),
         vm(20, 32, 128), vm(20, 32, 128), vm(20, 32, 128), vm(20, 32, 128), vm(20, 32, 128),
         vm(16, 128), vm(2, 3, 32, 128), vm(4, 32, 128),
-        vm(5, 8, 128), vm(sizes[0], 3, 5, 24, 128), vm(8, 128), vm(sizes[0], 3, 24, 128),
+        vm(5, 8, 128), vm(sizes[0], 5, 24, 128), vm(2, 2, 8, 128), vm(sizes[0], 2, 2, 24, 128),
+        vm(8, 128), vm(sizes[0], 3, 24, 128),
         vm(5, nx2, 24, 128), vm(nx2, 24, 128), vm(2, nx2, 24, 128), vm(nx2, 24, 128), vm(nx2, 24, 128),
         vm(nx2, 32, 128), vm(2, 12, 48, 128),
         vm(2, 6, 16, 128), vm(2, 6, 16, 128), vm(4, 8, 128), vm(4, 8, 128),

time: 53.5 us -> 51 us (0.953)
  Pallas kernels: 51.6 us -> 49.2 us
    pallas_call x1, Pallas kernels: 51.6 us -> 49.2 us  [local(): pl.pallas_call(functools.partial(kernel, sizes), out_shape=jax.ShapeDtype...]
where the time goes in v4:
time: 51 us; the launch traced here: 50.9 us
  Pallas kernels  49.2 us (96%)
  local copies, waits for them, and re-layouts  1.67 us (3%)
    pallas_call x1, Pallas kernels, local(): pl.pallas_call(functools.partial(kernel, sizes), out_shape=jax.ShapeDtype...  49.2 us
    unnamed x1, local copies, waits for them, and re-layouts  1.67 us

profile of v4, /device:TPU:1, one launch (start us, length us, event | category | flops | bytes accessed | tf_op | source)
XLA Modules:
  0.0 50.9 jit_solution(7849898386743971820)
XLA Ops:
  0.0 49.2 %vcycle.1 = f32[16,32,128]{2,1,0:T(8,128)} custom-call(f32[16,32,128]{2,1,0:T(8,128)} %b_in.1, f32[16,32,128]{2,1,0:T(8,128)} %fx_in.1, f32[16,32,128]{2,1,0:T(8,128)} %fy_in.1, f32[16,32,128]{2,1,0:T(8,128)} %fz_in.1, f32[16,32,128]{2,1,0:T(8,128)} %s_in.1), custom_call_target="tpu_custom_call" | custom-call | tf_op jit(solution)/shard_map/vcycle/pallas_call | solution.py:722
  49.2 1.7 %copy.7 = f32[16,32,128]{2,1,0:T(8,128)} copy(f32[16,32,128]{2,1,0:T(8,128)} %vcycle.1) | data formatting | bytes 524288
